TPU v7x, 32 devices: a whole 2x2x4 slice. The times are simulated.
32 devices in a mesh: tile: 16 (over z, x, core), split: 2 (over y).
Axes of the slice: x: 2, y: 2, z: 4, core: 2. Of those that a mesh axis runs over, the one named last changes fastest.
Arguments:
- noisy_image: bfloat16 [16, 45, 128, 128], P('tile', None, 'split'), may hold values from -60 to 60
- seam_codes: int32 [16, 4], replicated, may hold values from 0 to 3
- timestep: int32 [1], replicated, may hold values from 0 to 999
- time_weight: float32 [48, 192], replicated, may hold values from -0.875 to 0.875
- bias_upper: float32 [192, 48], replicated, may hold values from -0.875 to 0.875
- bias_lower: float32 [192, 96], replicated, may hold values from -0.875 to 0.875
- kernel_upper_first: bfloat16 [3, 3, 48, 45], replicated, may hold values from -0.3125 to 0.3125
- kernel_upper_second: bfloat16 [3, 3, 48, 48], replicated, may hold values from -0.3125 to 0.3125
- kernel_lower_first: bfloat16 [3, 3, 96, 48], replicated, may hold values from -0.3125 to 0.3125
- kernel_lower_second: bfloat16 [3, 3, 96, 96], replicated, may hold values from -0.21875 to 0.21875
- kernel_decode_first: bfloat16 [3, 3, 48, 144], replicated, may hold values from -0.15625 to 0.15625
- kernel_decode_second: bfloat16 [3, 3, 48, 48], replicated, may hold values from -0.3125 to 0.3125
- output_weight: bfloat16 [45, 48], replicated, may hold values from -0.875 to 0.875
- gains_upper: float32 [4, 48], replicated, may hold values from 0.25 to 1.75
- shifts_upper: float32 [4, 48], replicated, may hold values from -1 to 1
- gains_lower: float32 [2, 96], replicated, may hold values from 0.25 to 1.75
- shifts_lower: float32 [2, 96], replicated, may hold values from -1 to 1
Outputs:
- predicted_noise: bfloat16 [16, 45, 128, 128], P('tile', None, 'split')
All inputs are finite; a program needn't handle non-finite values.
Results may differ from a plain program's by a relative error of at most 0.018.
Values may be sent and summed in bfloat16 or wider, within the bound.
A program may use at most 128 MiB of HBM per device.

v0:
```python
import math

import jax
import jax.numpy as jnp
from jax import lax
from jax.sharding import PartitionSpec as P

GROUPS = 8
ROW_TILES = 4


EPSILON = 1e-05


def from_behind(value, axis, steps):
    count = lax.axis_size(axis)
    pairs = [(source, (source + steps) % count) for source in range(count)]
    return lax.ppermute(value, axis, pairs)


def apply_taps(padded, kernel, height, width):
    channels = padded.shape[0]
    outputs = kernel.shape[2]
    windows = []
    for row_off in range(3):
        for col_off in range(3):
            windows.append(
                padded[:, row_off : row_off + height, col_off : col_off + width].reshape(
                    channels, height * width
                )
            )
    stacked = jnp.concatenate(windows, axis=0)
    flat_kernel = jnp.transpose(kernel, (2, 0, 1, 3)).reshape(outputs, 9 * channels)
    total = jnp.dot(flat_kernel, stacked, preferred_element_type=jnp.float32)
    return total.reshape(outputs, height, width)


def framed_block(values, seam_codes):
    channels, block_rows, block_cols = values.shape
    split_count = lax.axis_size("split")
    split_place = lax.axis_index("split")
    tile_place = lax.axis_index("tile")
    top_rows, bottom_rows, left_cols, right_cols = (
        lax.all_gather(values[None, :, 0, :], "split", axis=0, tiled=True),
        lax.all_gather(values[None, :, block_rows - 1, :], "split", axis=0, tiled=True),
        lax.all_gather(values[None, :, :, 0], "split", axis=0, tiled=True),
        lax.all_gather(values[None, :, :, block_cols - 1], "split", axis=0, tiled=True),
    )
    west_full = jnp.transpose(left_cols, (1, 0, 2)).reshape(channels, block_cols)
    east_full = jnp.transpose(right_cols, (1, 0, 2)).reshape(channels, block_cols)
    sides = jnp.stack(
        [top_rows[0][:, ::-1], east_full[:, ::-1], bottom_rows[split_count - 1], west_full]
    )
    strip_list = []
    for side_index, offset in ((0, ROW_TILES), (1, -1), (2, -ROW_TILES), (3, 1)):
        received = from_behind(sides, "tile", offset)
        code_row = lax.dynamic_index_in_dim(seam_codes, tile_place, 0, False)
        facing = (side_index + 2 + code_row[side_index]) % 4
        strip_list.append(lax.dynamic_index_in_dim(received, facing, 0, False))
    north_strip = strip_list[0]
    east_strip = strip_list[1]
    south_strip = strip_list[2][:, ::-1]
    west_strip = strip_list[3][:, ::-1]
    above_row = lax.dynamic_index_in_dim(bottom_rows, jnp.maximum(split_place - 1, 0), 0, False)
    upper = jnp.where(split_place == 0, north_strip, above_row)
    below_row = lax.dynamic_index_in_dim(
        top_rows, jnp.minimum(split_place + 1, split_count - 1), 0, False
    )
    lower = jnp.where(split_place == split_count - 1, south_strip, below_row)
    west_column = lax.dynamic_slice_in_dim(
        jnp.pad(west_strip, ((0, 0), (1, 1))), split_place * block_rows, block_rows + 2, 1
    )
    east_column = lax.dynamic_slice_in_dim(
        jnp.pad(east_strip, ((0, 0), (1, 1))), split_place * block_rows, block_rows + 2, 1
    )
    stacked = jnp.concatenate([upper[:, None, :], values, lower[:, None, :]], axis=1)
    return jnp.concatenate([west_column[:, :, None], stacked, east_column[:, :, None]], axis=2)


def convolve(values, seam_codes, kernel):
    padded = framed_block(values, seam_codes)
    return apply_taps(padded, kernel, values.shape[1], values.shape[2])


def norm_act(values, gain, shift):
    grouped = values.reshape(GROUPS, -1)
    total = grouped.shape[1] * lax.axis_size("tile") * lax.axis_size("split")
    sums, squares = lax.psum(
        (jnp.sum(grouped, axis=1), jnp.sum(jnp.square(grouped), axis=1)), ("tile", "split")
    )
    mean = sums / total
    spread = squares / total - jnp.square(mean)
    normed = ((grouped - mean[:, None]) * lax.rsqrt(spread[:, None] + EPSILON)).reshape(
        values.shape
    )
    scaled = normed * gain[:, None, None] + shift[:, None, None]
    return jax.nn.silu(scaled).astype(jnp.bfloat16)


def embedding(timestep, time_weight, bias_upper, bias_lower):
    moment = timestep[0].astype(jnp.float32)
    half_width = time_weight.shape[0] // 2
    frequencies = jnp.exp(
        -math.log(10000.0) * jnp.arange(half_width, dtype=jnp.float32) / half_width
    )
    angles = moment * frequencies
    features = jnp.concatenate([jnp.sin(angles), jnp.cos(angles)])[None, :]
    embedded = jax.nn.silu(
        jnp.dot(
            features,
            time_weight,
            precision=lax.Precision.HIGHEST,
            preferred_element_type=jnp.float32,
        )
    )
    first_bias = jnp.dot(
        embedded, bias_upper, precision=lax.Precision.HIGHEST, preferred_element_type=jnp.float32
    )[0]
    second_bias = jnp.dot(
        embedded, bias_lower, precision=lax.Precision.HIGHEST, preferred_element_type=jnp.float32
    )[0]
    return (first_bias, second_bias)


def per_device(
    noisy_image,
    seam_codes,
    timestep,
    time_weight,
    bias_upper,
    bias_lower,
    kernel_upper_first,
    kernel_upper_second,
    kernel_lower_first,
    kernel_lower_second,
    kernel_decode_first,
    kernel_decode_second,
    output_weight,
    gains_upper,
    shifts_upper,
    gains_lower,
    shifts_lower,
):
    first_bias, second_bias = embedding(timestep, time_weight, bias_upper, bias_lower)
    image = noisy_image[0]
    first = norm_act(
        convolve(image, seam_codes, kernel_upper_first) + first_bias[:, None, None],
        gains_upper[0],
        shifts_upper[0],
    )
    skip = norm_act(
        convolve(first, seam_codes, kernel_upper_second), gains_upper[1], shifts_upper[1]
    )
    width_one, block_rows, block_cols = skip.shape
    pooled = jnp.mean(
        skip.astype(jnp.float32).reshape(width_one, block_rows // 2, 2, block_cols // 2, 2),
        axis=(2, 4),
    ).astype(jnp.bfloat16)
    middle = norm_act(
        convolve(pooled, seam_codes, kernel_lower_first) + second_bias[:, None, None],
        gains_lower[0],
        shifts_lower[0],
    )
    deep = norm_act(
        convolve(middle, seam_codes, kernel_lower_second), gains_lower[1], shifts_lower[1]
    )
    widened = jnp.repeat(jnp.repeat(deep, 2, axis=1), 2, axis=2)
    joined = jnp.concatenate([widened, skip], axis=0)
    decoded = norm_act(
        convolve(joined, seam_codes, kernel_decode_first), gains_upper[2], shifts_upper[2]
    )
    refined = norm_act(
        convolve(decoded, seam_codes, kernel_decode_second), gains_upper[3], shifts_upper[3]
    )
    flat = jnp.dot(
        output_weight,
        refined.reshape(width_one, block_rows * block_cols),
        preferred_element_type=jnp.float32,
    )
    return flat.reshape(output_weight.shape[0], block_rows, block_cols).astype(jnp.bfloat16)[None]


def solution(mesh):
    placed = (
        P("tile", None, "split", None),
        P(),
        P(),
        P(),
        P(),
        P(),
        P(),
        P(),
        P(),
        P(),
        P(),
        P(),
        P(),
        P(),
        P(),
        P(),
        P(),
    )
    return jax.shard_map(
        per_device,
        mesh=mesh,
        in_specs=placed,
        out_specs=P("tile", None, "split", None),
        check_vma=False,
    )
```

profile of v0, /device:TPU:0, one launch (start us, length us, event | category | flops | bytes accessed | tf_op | source)
XLA Modules:
  0.0 781.5 jit_solution(2221775339803490812)
XLA Ops:
  2.8 5.5 all-gather
  51.6 55.5 %concatenate.153 = bf16[405,8192]{1,0:T(8,128)(2,1)} concatenate(bf16[45,8192]{1,0:T(8,128)(2,1)} %bitcast.537, bf16[45,8192]{1,0:T(8,128)(2,1)S(1)} %bitcast.533, bf16[45,8192]{1,0:T(8,128)(2,1)} %bitcast.536, bf16[45,8192]{1,0:T(8,128)(2,1)} %bitcast.538, bf16[45,8192]{1,0:T(8,128)(2,1)S(1)} %bitcast.531, bf16[45,8192]{1,0:T(8,128)(2,1)} %bitcast.535, ...), dimensions={0} | concatenate | bytes 13271040 | tf_op jit(solution)/shard_map/concatenate | solution.py:32
  112.4 40.2 %all-reduce.17 = (f32[8]{0:T(128)S(1)}, f32[8]{0:T(128)S(1)}) all-reduce(f32[8]{0:T(128)S(1)} %reduce_sum.157, f32[8]{0:T(128)S(1)} %reduce_sum.151), channel_id=1, replica_groups=mesh['tile'=16,'split'=2] {'tile','split'}, use_global_device_ids=true, to_apply=%region_5.6 | all-reduce | flops 16 | bytes 128 | tf_op jit(solution)/shard_map/psum | solution.py:88
  165.7 20.8 %all-gather.5 = bf16[96,64,1]{2,0,1:T(8,128)(2,1)} all-gather(bf16[48,64,1]{2,0,1:T(8,128)(2,1)} %get-tuple-element.69), channel_id=7, replica_groups=mesh['tile'=16,'split'=2] {'split'}, dimensions={0}, use_global_device_ids=true | all-gather | bytes 18432 | tf_op jit(solution)/shard_map/all_gather | solution.py:47
  189.7 16.5 %all-gather.7 = bf16[96,64,1]{2,0,1:T(8,128)(2,1)} all-gather(bf16[48,64,1]{2,0,1:T(8,128)(2,1)S(1)} %get-tuple-element.70), channel_id=9, replica_groups=mesh['tile'=16,'split'=2] {'split'}, dimensions={0}, use_global_device_ids=true | all-gather | bytes 18432 | tf_op jit(solution)/shard_map/all_gather | solution.py:46
  232.6 37.4 %all-reduce.16 = (f32[8]{0:T(128)S(1)}, f32[8]{0:T(128)S(1)}) all-reduce(f32[8]{0:T(128)S(1)} %reduce_sum.166, f32[8]{0:T(128)S(1)} %reduce_sum.163), channel_id=1, replica_groups=mesh['tile'=16,'split'=2] {'tile','split'}, use_global_device_ids=true, to_apply=%region_11.12 | all-reduce | flops 16 | bytes 128 | tf_op jit(solution)/shard_map/psum | solution.py:88
  272.9 7.1 copy.764
  280.1 5.2 convert_reduce_fusion
  334.6 37.2 %all-reduce.15 = (f32[8]{0:T(128)S(1)}, f32[8]{0:T(128)S(1)}) all-reduce(f32[8]{0:T(128)S(1)} %reduce_sum.179, f32[8]{0:T(128)S(1)} %reduce_sum.173), channel_id=1, replica_groups=mesh['tile'=16,'split'=2] {'tile','split'}, use_global_device_ids=true, to_apply=%region_18.19 | all-reduce | flops 16 | bytes 128 | tf_op jit(solution)/shard_map/psum | solution.py:88
  373.0 5.0 all-gather.12
  378.3 4.8 all-gather.14
  383.4 5.1 all-gather.13
  418.3 37.8 %all-reduce.14 = (f32[8]{0:T(128)S(1)}, f32[8]{0:T(128)S(1)}) all-reduce(f32[8]{0:T(128)S(1)} %reduce_sum.225, f32[8]{0:T(128)S(1)} %reduce_sum.182), channel_id=1, replica_groups=mesh['tile'=16,'split'=2] {'tile','split'}, use_global_device_ids=true, to_apply=%region_24.25 | all-reduce | flops 16 | bytes 128 | tf_op jit(solution)/shard_map/psum | solution.py:88
  463.2 5.3 all-gather.17
  470.6 5.0 all-gather.19
  482.6 4.8 all-gather.18
  504.8 9.8 %pad_maximum_fusion.1 = (bf16[144,64,128]{0,1,2:T(8,128)(2,1)}, bf16[144,64,128]{0,1,2:T(8,128)(2,1)}) fusion(bf16[144,1,128]{0,1,2:T(2,128)(2,1)S(1)} %copy.832, bf16[48,64,128]{0,1,2:T(8,128)(2,1)S(1)} %copy.822, bf16[96,64,128]{0,1,2:T(8,128)(2,1)} %bitcast.498, bf16[144,1,128]{0,1,2:T(2,128)(2,1)S(1)} %copy.831), kind=kLoop, calls=%fused_computation.3 | loop fusion | flops 14155776 | bytes 7151616 | tf_op jit(solution)/shard_map/concatenate | solution.py:76
  514.6 7.0 copy.843
  521.6 7.0 copy.836
  528.6 14.0 %pad_maximum_fusion = (bf16[144,66,129]{0,1,2:T(8,128)(2,1)S(1)}, bf16[144,66,129]{0,1,2:T(8,128)(2,1)}) fusion(bf16[144,66,1]{0,1,2:T(8,128)(2,1)S(1)} %copy.837, bf16[144,1,128]{0,1,2:T(2,128)(2,1)S(1)} %copy.832, bf16[48,64,128]{0,1,2:T(8,128)(2,1)S(1)} %copy.822, bf16[96,64,128]{0,1,2:T(8,128)(2,1)} %bitcast.499, bf16[144,1,128]{0,1,2:T(2,128)(2,1)S(1)} %copy.831, ...), kind=kLoop, calls=%fused_computation.2 | loop fusion | flops 24520320 | bytes 7375104 | tf_op jit(solution)/shard_map/concatenate | solution.py:77
  542.6 7.3 fusion.77
  549.9 8.2 %copy.844 = bf16[144,64,128]{2,1,0:T(8,128)(2,1)S(1)} copy(bf16[144,64,128]{0,1,2:T(8,128)(2,1)} %get-tuple-element.23) | data formatting | bytes 4718592 | tf_op jit(solution)/shard_map/slice | solution.py:28
  558.1 7.0 copy.840
  565.1 7.2 copy.838
  572.3 10.6 %fusion.78 = (bf16[144,64,128]{0,1,2:T(8,128)(2,1)}, bf16[144,64,128]{0,1,2:T(8,128)(2,1)}, bf16[144,64,128]{0,1,2:T(8,128)(2,1)}) fusion(bf16[144,66,129]{0,1,2:T(8,128)(2,1)} %get-tuple-element.30), kind=kLoop, calls=%fused_computation.283 | loop fusion | bytes 14155776 | tf_op jit(solution)/shard_map/slice | solution.py:28
  582.9 7.0 copy.841
  589.9 7.0 copy.839
  596.9 7.0 copy.834
  629.2 40.0 %all-reduce.13 = (f32[8]{0:T(128)S(1)}, f32[8]{0:T(128)S(1)}) all-reduce(f32[8]{0:T(128)S(1)} %reduce_sum.231, f32[8]{0:T(128)S(1)} %reduce_sum.228), channel_id=1, replica_groups=mesh['tile'=16,'split'=2] {'tile','split'}, use_global_device_ids=true, to_apply=%region_30.31 | all-reduce | flops 16 | bytes 128 | tf_op jit(solution)/shard_map/psum | solution.py:88
  680.5 20.9 %all-gather.21 = bf16[96,64,1]{2,0,1:T(8,128)(2,1)} all-gather(bf16[48,64,1]{2,0,1:T(8,128)(2,1)} %get-tuple-element.63), channel_id=23, replica_groups=mesh['tile'=16,'split'=2] {'split'}, dimensions={0}, use_global_device_ids=true | all-gather | bytes 18432 | tf_op jit(solution)/shard_map/all_gather | solution.py:47
  704.1 16.5 %all-gather.23 = bf16[96,64,1]{2,0,1:T(8,128)(2,1)} all-gather(bf16[48,64,1]{2,0,1:T(8,128)(2,1)S(1)} %get-tuple-element.64), channel_id=25, replica_groups=mesh['tile'=16,'split'=2] {'split'}, dimensions={0}, use_global_device_ids=true | all-gather | bytes 18432 | tf_op jit(solution)/shard_map/all_gather | solution.py:46
  741.6 37.4 %all-reduce.12 = (f32[8]{0:T(128)S(1)}, f32[8]{0:T(128)S(1)}) all-reduce(f32[8]{0:T(128)S(1)} %reduce_sum.237, f32[8]{0:T(128)S(1)} %reduce_sum.234), channel_id=1, replica_groups=mesh['tile'=16,'split'=2] {'tile','split'}, use_global_device_ids=true, to_apply=%region_36.37 | all-reduce | flops 16 | bytes 128 | tf_op jit(solution)/shard_map/psum | solution.py:88
  (596 shorter events, 268.7 us)
Async XLA Ops:
  0.0 332.1 %copy-start = (bf16[3,3,96,48]{2,3,1,0:T(8,128)(2,1)S(1)}, bf16[3,3,96,48]{2,3,1,0:T(8,128)(2,1)}, u32[]{:S(2)}) copy-start(bf16[3,3,96,48]{2,3,1,0:T(8,128)(2,1)} %param.25) | copy-start | bytes 248836
  23.4 11.2 %collective-permute-start.3 = (bf16[4,45,128]{2,1,0:T(8,128)(2,1)S(1)}, bf16[4,45,128]{2,1,0:T(8,128)(2,1)S(1)}, u32[]{:S(2)}, u32[]{:S(2)}) collective-permute-start(bf16[4,45,128]{2,1,0:T(8,128)(2,1)S(1)} %pad_maximum_fusion.25), channel_id=1, source_target_pairs={{0,30},{2,0},{4,2},{6,4},{8,6},{10,8},{12,10},{14,12},{16,14},{18,... | collective-permute-start | bytes 138248 | tf_op jit(solution)/shard_map/ppermute | solution.py:18
  23.5 10.4 %collective-permute-start.2 = (bf16[4,45,128]{2,1,0:T(8,128)(2,1)S(1)}, bf16[4,45,128]{2,1,0:T(8,128)(2,1)S(1)}, u32[]{:S(2)}, u32[]{:S(2)}) collective-permute-start(bf16[4,45,128]{2,1,0:T(8,128)(2,1)S(1)} %pad_maximum_fusion.25), channel_id=1, source_target_pairs={{0,24},{2,26},{4,28},{6,30},{8,0},{10,2},{12,4},{14,6},{16,8},{18,... | collective-permute-start | bytes 138248 | tf_op jit(solution)/shard_map/ppermute | solution.py:18
  27.7 6.8 collective-permute-start.1
  27.7 6.8 collective-permute-start
  29.6 123.3 %copy-start.52 = (f32[48]{0:T(128)}, f32[48]{0:T(128)S(1)}, u32[]{:S(2)}) copy-start(f32[48]{0:T(128)S(1)} %get-tuple-element.113) | copy-start | bytes 580
  29.6 123.3 %copy-start.54 = (f32[48]{0:T(128)}, f32[48]{0:T(128)S(1)}, u32[]{:S(2)}) copy-start(f32[48]{0:T(128)S(1)} %get-tuple-element.150) | copy-start | bytes 580
  210.4 6.2 collective-permute-start.7
  214.0 4.7 collective-permute-start.6
  216.3 8.9 %collective-permute-start.5 = (bf16[4,48,128]{2,1,0:T(8,128)(2,1)}, bf16[4,48,128]{2,1,0:T(8,128)(2,1)S(1)}, u32[]{:S(2)}, u32[]{:S(2)}) collective-permute-start(bf16[4,48,128]{2,1,0:T(8,128)(2,1)} %pad_maximum_fusion.26), channel_id=1, source_target_pairs={{0,8},{2,10},{4,12},{6,14},{8,16},{10,18},{12,20},{14,22},{16,24},... | collective-permute-start | bytes 147464 | tf_op jit(solution)/shard_map/ppermute | solution.py:18
  216.3 6.4 collective-permute-start.4
  231.9 101.1 %copy-start.3 = (f32[8192,48]{0,1:T(8,128)}, f32[8192,48]{0,1:T(8,128)S(1)}, u32[]{:S(2)}) copy-start(f32[8192,48]{0,1:T(8,128)S(1)} %get-tuple-element.137) | copy-start | bytes 4718596
  306.1 6.5 collective-permute-start.11
  306.6 5.8 collective-permute-start.10
  308.5 6.4 collective-permute-start.9
  309.1 8.0 %collective-permute-start.8 = (bf16[4,48,64]{1,2,0:T(8,128)(2,1)S(1)}, bf16[4,48,64]{1,2,0:T(8,128)(2,1)S(1)}, u32[]{:S(2)}, u32[]{:S(2)}) collective-permute-start(bf16[4,48,64]{1,2,0:T(8,128)(2,1)S(1)} %pad_maximum_fusion.23), channel_id=1, source_target_pairs={{0,2},{2,4},{4,6},{6,8},{8,10},{10,12},{12,14},{14,16},{16,18},{18... | collective-permute-start | bytes 73736 | tf_op jit(solution)/shard_map/ppermute | solution.py:18
  393.8 3.0 collective-permute-start.15
  393.9 5.9 collective-permute-start.14
  396.2 7.9 %collective-permute-start.13 = (bf16[4,96,64]{1,2,0:T(8,128)(2,1)S(1)}, bf16[4,96,64]{1,2,0:T(8,128)(2,1)S(1)}, u32[]{:S(2)}, u32[]{:S(2)}) collective-permute-start(bf16[4,96,64]{1,2,0:T(8,128)(2,1)S(1)} %pad_maximum_fusion.24), channel_id=1, source_target_pairs={{0,8},{2,10},{4,12},{6,14},{8,16},{10,18},{12,20},{14,22},{16,24},... | collective-permute-start | bytes 147464 | tf_op jit(solution)/shard_map/ppermute | solution.py:18
  396.4 7.6 collective-permute-start.12
  414.4 43.4 %copy-start.64 = (f32[96]{0:T(128)S(1)}, f32[96]{0:T(128)}, u32[]{:S(2)}) copy-start(f32[96]{0:T(128)} %get-tuple-element.121) | copy-start | bytes 1156
  414.4 43.4 %copy-start.65 = (f32[96]{0:T(128)S(1)}, f32[96]{0:T(128)}, u32[]{:S(2)}) copy-start(f32[96]{0:T(128)} %get-tuple-element.154) | copy-start | bytes 1156
  488.9 12.4 %collective-permute-start.18 = (bf16[4,144,128]{2,1,0:T(8,128)(2,1)}, bf16[4,144,128]{2,1,0:T(8,128)(2,1)}, u32[]{:S(2)}, u32[]{:S(2)}) collective-permute-start(bf16[4,144,128]{2,1,0:T(8,128)(2,1)} %pad_maximum_fusion.20), channel_id=1, source_target_pairs={{0,24},{2,26},{4,28},{6,30},{8,0},{10,2},{12,4},{14,6},{16,8},{18,... | collective-permute-start | bytes 442376 | tf_op jit(solution)/shard_map/ppermute | solution.py:18
  493.0 9.3 %collective-permute-start.19 = (bf16[4,144,128]{2,1,0:T(8,128)(2,1)}, bf16[4,144,128]{2,1,0:T(8,128)(2,1)}, u32[]{:S(2)}, u32[]{:S(2)}) collective-permute-start(bf16[4,144,128]{2,1,0:T(8,128)(2,1)} %pad_maximum_fusion.20), channel_id=1, source_target_pairs={{0,30},{2,0},{4,2},{6,4},{8,6},{10,8},{12,10},{14,12},{16,14},{18,... | collective-permute-start | bytes 442376 | tf_op jit(solution)/shard_map/ppermute | solution.py:18
  493.0 10.4 %collective-permute-start.17 = (bf16[4,144,128]{2,1,0:T(8,128)(2,1)}, bf16[4,144,128]{2,1,0:T(8,128)(2,1)S(1)}, u32[]{:S(2)}, u32[]{:S(2)}) collective-permute-start(bf16[4,144,128]{2,1,0:T(8,128)(2,1)} %pad_maximum_fusion.20), channel_id=1, source_target_pairs={{0,8},{2,10},{4,12},{6,14},{8,16},{10,18},{12,20},{14,22},{16,24},... | collective-permute-start | bytes 442376 | tf_op jit(solution)/shard_map/ppermute | solution.py:18
  493.0 11.3 %collective-permute-start.16 = (bf16[4,144,128]{2,1,0:T(8,128)(2,1)}, bf16[4,144,128]{2,1,0:T(8,128)(2,1)S(1)}, u32[]{:S(2)}, u32[]{:S(2)}) collective-permute-start(bf16[4,144,128]{2,1,0:T(8,128)(2,1)} %pad_maximum_fusion.20), channel_id=1, source_target_pairs={{0,2},{2,4},{4,6},{6,8},{8,10},{10,12},{12,14},{14,16},{16,18},{18... | collective-permute-start | bytes 442376 | tf_op jit(solution)/shard_map/ppermute | solution.py:18
  624.6 45.0 %copy-start.62 = (f32[48]{0:T(128)S(1)}, f32[48]{0:T(128)}, u32[]{:S(2)}) copy-start(f32[48]{0:T(128)} %get-tuple-element.114) | copy-start | bytes 580
  624.6 45.0 %copy-start.63 = (f32[48]{0:T(128)S(1)}, f32[48]{0:T(128)}, u32[]{:S(2)}) copy-start(f32[48]{0:T(128)} %get-tuple-element.149) | copy-start | bytes 580
  723.4 3.1 collective-permute-start.23
  723.7 4.7 collective-permute-start.22
  726.3 8.7 %collective-permute-start.21 = (bf16[4,48,128]{2,1,0:T(8,128)(2,1)S(1)}, bf16[4,48,128]{2,1,0:T(8,128)(2,1)S(1)}, u32[]{:S(2)}, u32[]{:S(2)}) collective-permute-start(bf16[4,48,128]{2,1,0:T(8,128)(2,1)S(1)} %pad_maximum_fusion.27), channel_id=1, source_target_pairs={{0,8},{2,10},{4,12},{6,14},{8,16},{10,18},{12,20},{14,22},{16,24},... | collective-permute-start | bytes 147464 | tf_op jit(solution)/shard_map/ppermute | solution.py:18
  726.3 6.2 collective-permute-start.20
  (66 other events, 641.2 us)
where the time goes:
time: 793 us; the launch traced here: 781 us
  blocking collectives  399 us (50%)
  local copies, waits for them, and re-layouts  265 us (33%)
  other arithmetic  50.8 us (6%)
  waiting for transfers between devices  27.1 us (3%)
  starting transfers between devices  18.5 us (2%)
  matrix products  15.6 us (2%)
    psum x6, blocking collectives, norm_act(): lax.psum((jnp.sum(grouped, axis=1), jnp.sum(jnp.square(grouped), axis=1))...  230 us
    slice x15, local copies, waits for them, and re-layouts, apply_taps(): padded[:, row_off:row_off + height, col_off:col_off + width]  79.6 us
    all_gather x6, blocking collectives, framed_block(): lax.all_gather(values[None, :, :, block_cols - 1], 'split', axis=0, tiled...  61.3 us
    concatenate x6, local copies, waits for them, and re-layouts, apply_taps(): stacked = jnp.concatenate(windows, axis=0)  57.6 us
    all_gather x6, blocking collectives, framed_block(): lax.all_gather(values[None, :, :, 0], 'split', axis=0, tiled=True)  51.8 us
    unnamed x218, local copies, waits for them, and re-layouts  43.4 us
    all_gather x6, blocking collectives, framed_block(): lax.all_gather(values[None, :, 0, :], 'split', axis=0, tiled=True)  28.9 us
    all_gather x6, blocking collectives, framed_block(): lax.all_gather(values[None, :, block_rows - 1, :], 'split', axis=0, tiled...  27.2 us
  transfers between devices with their start and end apart: 24, of which 11 were waited for; matrix products, arithmetic and copies ran while one was open for 3% of the time, Pallas kernels for 0%

commit v1 on v0

v1 whole, which is shorter than its diff:
```python
import functools
import math

import jax
import jax.numpy as jnp
from jax import lax
from jax.experimental import pallas as pl
from jax.experimental.pallas import tpu as pltpu
from jax.sharding import PartitionSpec as P

GROUPS = 8
ROW_TILES = 4
EPSILON = 1e-05
LANES = 128
MESH = pl.DeviceIdType.MESH
F32 = jnp.float32
BF16 = jnp.bfloat16
HIGH = lax.Precision.HIGHEST


def lanes_of(channels):
    return lax.broadcasted_iota(jnp.int32, (channels, LANES), 1)


def kernel(
    tiles, one, two, rows, cols, outputs,
    codes, image, params, w_uf, w_us, w_lf, w_ls, w_df, w_ds, w_out,
    out,
    x_one, x_low, x_mid, x_join, raw_up, raw_low, pool_ref, stats, stats_in, stats_two, stats_two_in, *rest,
):
    sends, recvs, inners = rest[0:7], rest[7:14], rest[14:21]
    send_sem, recv_sem, stat_send, stat_recv = rest[21:25]
    t, s = lax.axis_index("tile"), lax.axis_index("split")
    a, b = lax.div(t, ROW_TILES), lax.rem(t, ROW_TILES)
    depth = tiles // ROW_TILES
    plane = 2 * ROW_TILES
    half_rows, half_cols = rows // 2, cols // 2

    def across(offset):
        return lax.rem(t + offset + tiles, tiles)

    def plane_peer(step):
        place = lax.rem(b * 2 + s + step, plane)
        return (a * ROW_TILES + lax.div(place, 2), lax.rem(place, 2))

    def depth_peer(step):
        return (lax.rem(a + step, depth) * ROW_TILES + b, s)

    peers = [plane_peer(step) for step in range(1, plane)]
    peers += [depth_peer(step) for step in range(1, depth)]
    for offset in (ROW_TILES, -ROW_TILES, 1, -1):
        peers += [(across(offset), 0), (across(offset), 1)]
    barrier = pltpu.get_barrier_semaphore()
    for peer in peers:
        pl.semaphore_signal(barrier, inc=1, device_id=peer, device_id_type=MESH)
    pl.semaphore_wait(barrier, len(peers))

    def halo_copies(e):
        send, recv, inner = sends[e], recvs[e], inners[e]
        targets = [
            (0, (across(ROW_TILES), 0)), (0, (across(-ROW_TILES), 1)),
            (2, (across(-1), 0)), (2, (across(-1), 1)),
            (4, (across(1), 0)), (4, (across(1), 1)),
        ]
        copies = []
        for n, (slot, peer) in enumerate(targets):
            copies.append(pltpu.make_async_remote_copy(
                src_ref=send.at[pl.ds(0, 2)], dst_ref=recv.at[slot + s],
                send_sem=send_sem.at[e, n], recv_sem=recv_sem.at[e, slot + s],
                device_id=peer, device_id_type=MESH))
        copies.append(pltpu.make_async_remote_copy(
            src_ref=send.at[2], dst_ref=inner,
            send_sem=send_sem.at[e, 6], recv_sem=recv_sem.at[e, 6],
            device_id=(t, 1 - s), device_id_type=MESH))
        return copies

    def halo_start(e, top, bottom, columns):
        first = jnp.full(top.shape, s, jnp.int32) == 0
        sends[e][0] = jnp.where(first, top, bottom).astype(BF16)
        sends[e][1] = columns.astype(BF16)
        sends[e][2] = jnp.where(first, bottom, top).astype(BF16)
        for copy in halo_copies(e):
            copy.start()

    def halo_wait(e):
        send, recv, inner = sends[e], recvs[e], inners[e]
        for n in range(6):
            pltpu.make_async_remote_copy(
                src_ref=send.at[pl.ds(0, 2)], dst_ref=recv.at[n],
                send_sem=send_sem.at[e, n], recv_sem=recv_sem.at[e, n],
                device_id=(t, 1 - s), device_id_type=MESH).wait()
        pltpu.make_async_remote_copy(
            src_ref=send.at[2], dst_ref=inner,
            send_sem=send_sem.at[e, 6], recv_sem=recv_sem.at[e, 6],
            device_id=(t, 1 - s), device_id_type=MESH).wait()

    def mover(flip, off, wide, up):
        i = lax.broadcasted_iota(jnp.int32, (LANES, LANES), 0)
        p = lax.broadcasted_iota(jnp.int32, (LANES, LANES), 1) + off
        index = p + flip * (wide - 1 - 2 * p)
        if up:
            hit = (i * 2 == index) | (i * 2 + 1 == index)
        else:
            hit = i == index
        return jnp.where(hit & (p >= 0) & (p < wide), 1.0, 0.0).astype(BF16)

    def halo_finish(e, height, act, up):
        halo_wait(e)
        recv = recvs[e]
        channels = recv.shape[2]
        lane = lanes_of(channels)
        scale = 2 if up else 1
        tall, wide = height * scale, height * 2 * scale
        strips = []
        for place, side in ((0, 2 * s), (2, 1), (4, 3)):
            k = lax.rem(side + 2 + codes[t, side], 4)
            kv = jnp.full((channels, LANES), k, jnp.int32)
            zero, last = recv[place, 0].astype(F32), recv[place + 1, 0].astype(F32)
            col0, col1 = recv[place, 1].astype(F32), recv[place + 1, 1].astype(F32)
            upper_half = lane < height
            left = jnp.where(upper_half, col0, pltpu.roll(col1, height, 1))
            shift = (height - 64) % LANES
            right = jnp.where(
                upper_half, pltpu.roll(col0, 64, 1), pltpu.roll(col1, shift, 1) if shift else col1)
            cand = jnp.where(kv == 0, zero, jnp.where(kv == 1, right, jnp.where(kv == 2, last, left)))
            reverse = 1 if place == 4 else (s if place == 0 else 0)
            front = jnp.where(k < 2, 1, 0)
            flip = front + reverse - 2 * front * reverse
            off = 0 if place == 0 else s * tall - 1
            strips.append(jnp.dot(act(cand).astype(BF16), mover(flip, off, wide, up),
                                  preferred_element_type=F32))
        inner = act(inners[e][...].astype(F32)).astype(BF16)
        if up:
            inner = jnp.dot(inner, mover(0, 0, wide, True), preferred_element_type=F32)
        else:
            inner = inner.astype(F32)
        first = jnp.full((channels, LANES), s, jnp.int32) == 0
        upper = jnp.where(first, strips[0], inner)
        lower = jnp.where(first, inner, strips[0])
        return upper, lower, strips[2], strips[1]

    def put(ref, where_rows, j, y, west, east, wide, base, stride):
        channels = y.shape[0]
        lane = lanes_of(channels)
        left = jnp.where(lane == 0, pltpu.roll(west, lax.rem(LANES - j, LANES), 1), pltpu.roll(y, 1, 1))
        right = jnp.where(lane == wide - 1, pltpu.roll(east, wide - 1 - j, 1), pltpu.roll(y, LANES - 1, 1))
        left, mid, right = left.astype(BF16), y.astype(BF16), right.astype(BF16)
        for row in where_rows:
            ref[row, pl.ds(base, channels), :] = left
            ref[row, pl.ds(stride + base, channels), :] = mid
            ref[row, pl.ds(2 * stride + base, channels), :] = right

    def columns_with(columns, o, h, wide):
        lane = lanes_of(o.shape[0])
        columns = jnp.where(lane == h, pltpu.roll(o, h, 1), columns)
        return jnp.where(lane == 64 + h, pltpu.roll(o, lax.rem(64 + h + LANES - wide + 1, LANES), 1), columns)

    def conv(x_ref, w_ref, raw, height, wide, bias):
        outs = w_ref.shape[0]
        taps = 3 * x_ref.shape[1]

        def body(i, carry):
            acc, acc2, columns = carry
            for pair in range(2):
                h = i * 4 + pair * 2
                x = jnp.concatenate(
                    [x_ref[pl.ds(h, 3)].reshape(taps, LANES), x_ref[pl.ds(h + 1, 3)].reshape(taps, LANES)], axis=1)
                o = jnp.dot(w_ref[...], x, preferred_element_type=F32)
                for n in range(2):
                    part = o[:, n * LANES:(n + 1) * LANES]
                    if bias is not None:
                        part = part + bias
                    raw[h + n] = part
                    acc = acc + part
                    acc2 = acc2 + part * part
                    columns = columns_with(columns, part, h + n, wide)
            return acc, acc2, columns

        zero = jnp.zeros((outs, LANES), F32)
        return lax.fori_loop(0, height // 4, body, (zero, zero, zero))

    def reduce_stats(e, acc, acc2, height, wide, gain, shift):
        channels = acc.shape[0]
        size = channels // GROUPS
        g = lax.broadcasted_iota(jnp.int32, (GROUPS, channels), 0)
        c = lax.broadcasted_iota(jnp.int32, (GROUPS, channels), 1)
        member = jnp.where((c >= g * size) & (c < g * size + size), 1.0, 0.0).astype(F32)
        gt = lax.broadcasted_iota(jnp.int32, (channels, GROUPS), 1)
        ct = lax.broadcasted_iota(jnp.int32, (channels, GROUPS), 0)
        spread_out = jnp.where((ct >= gt * size) & (ct < gt * size + size), 1.0, 0.0).astype(F32)
        stats[e, pl.ds(0, GROUPS)] = jnp.dot(member, acc, precision=HIGH, preferred_element_type=F32)
        stats[e, pl.ds(GROUPS, GROUPS)] = jnp.dot(member, acc2, precision=HIGH, preferred_element_type=F32)
        copies = []
        for step in range(1, plane):
            copies.append(pltpu.make_async_remote_copy(
                src_ref=stats.at[e], dst_ref=stats_in.at[e, step],
                send_sem=stat_send.at[e, step], recv_sem=stat_recv.at[e, step],
                device_id=plane_peer(step), device_id_type=MESH))
        for copy in copies:
            copy.start()
        total = stats[e]
        for step, copy in enumerate(copies):
            copy.wait()
            total = total + stats_in[e, step + 1]
        stats_two[e] = total
        copies = []
        for step in range(1, depth):
            copies.append(pltpu.make_async_remote_copy(
                src_ref=stats_two.at[e], dst_ref=stats_two_in.at[e, step],
                send_sem=stat_send.at[e, plane + step], recv_sem=stat_recv.at[e, plane + step],
                device_id=depth_peer(step), device_id_type=MESH))
        for copy in copies:
            copy.start()
        for step, copy in enumerate(copies):
            copy.wait()
            total = total + stats_two_in[e, step + 1]
        total = jnp.where(lanes_of(2 * GROUPS) < wide, total, 0.0)
        means = jnp.sum(total, axis=1, keepdims=True) * (1.0 / (height * wide * size * 2 * tiles))
        mean = means[:GROUPS]
        inverse = lax.rsqrt(means[GROUPS:] - mean * mean + EPSILON)
        mean = jnp.broadcast_to(mean, (GROUPS, LANES))
        inverse = jnp.broadcast_to(inverse, (GROUPS, LANES))
        mean = jnp.dot(spread_out, mean, precision=HIGH, preferred_element_type=F32)
        inverse = jnp.dot(spread_out, inverse, precision=HIGH, preferred_element_type=F32)
        slope = 0.5 * gain * inverse
        offset = 0.5 * shift - mean * slope

        def act(u):
            y = u * slope + offset
            return y + y * jnp.tanh(y)
        return act

    def column(index, channels):
        return jnp.broadcast_to(params[pl.ds(0, channels), pl.ds(index, 1)], (channels, LANES))

    def same(value):
        return value

    def fill_edges(ref, height, wide, edges, base, stride):
        upper, lower, west, east = edges
        put(ref, [0], 0, upper, west, east, wide, base, stride)
        put(ref, [height + 1], height + 1, lower, west, east, wide, base, stride)

    def image_columns(h, columns):
        return columns_with(columns, image[h].astype(F32), h, cols)

    columns = lax.fori_loop(0, rows, image_columns, jnp.zeros((one, LANES), F32))
    halo_start(0, image[0].astype(F32), image[rows - 1].astype(F32), columns)
    edges = halo_finish(0, rows, same, False)
    fill_edges(x_one, rows, cols, edges, 0, one)

    def fill_image(h, c):
        put(x_one, [h + 1], h + 1, image[h].astype(F32), edges[2], edges[3], cols, 0, one)
        return c
    lax.fori_loop(0, rows, fill_image, 0)

    acc, acc2, columns = conv(x_one, w_uf, raw_up, rows, cols, column(12, one))
    halo_start(1, raw_up[0], raw_up[rows - 1], columns)
    act = reduce_stats(0, acc, acc2, rows, cols, column(0, one), column(4, one))
    edges = halo_finish(1, rows, act, False)
    fill_edges(x_one, rows, cols, edges, 0, one)

    def fill_first(h, c):
        put(x_one, [h + 1], h + 1, act(raw_up[h]), edges[2], edges[3], cols, 0, one)
        return c
    lax.fori_loop(0, rows, fill_first, 0)

    acc, acc2, columns = conv(x_one, w_us, raw_up, rows, cols, None)
    halo_start(2, raw_up[0], raw_up[rows - 1], columns)
    act_skip = reduce_stats(1, acc, acc2, rows, cols, column(1, one), column(5, one))
    skip_edges = halo_finish(2, rows, act_skip, False)
    fill_edges(x_join, rows, cols, skip_edges, two, one + two)
    i = lax.broadcasted_iota(jnp.int32, (LANES, LANES), 0)
    j = lax.broadcasted_iota(jnp.int32, (LANES, LANES), 1)
    pooling = jnp.where((i == 2 * j) | (i == 2 * j + 1), 0.25, 0.0).astype(BF16)

    def fill_skip(h, columns):
        pooled = jnp.zeros((one, LANES), F32)
        for n in range(2):
            y = act_skip(raw_up[2 * h + n])
            put(x_join, [2 * h + n + 1], 2 * h + n + 1, y, skip_edges[2], skip_edges[3], cols, two, one + two)
            pooled = pooled + jnp.dot(y.astype(BF16), pooling, preferred_element_type=F32)
        pool_ref[h] = pooled
        return columns_with(columns, pooled, h, half_cols)
    columns = lax.fori_loop(0, half_rows, fill_skip, jnp.zeros((one, LANES), F32))
    halo_start(3, pool_ref[0], pool_ref[half_rows - 1], columns)
    edges = halo_finish(3, half_rows, same, False)
    fill_edges(x_low, half_rows, half_cols, edges, 0, one)

    def fill_pooled(h, c):
        put(x_low, [h + 1], h + 1, pool_ref[h], edges[2], edges[3], half_cols, 0, one)
        return c
    lax.fori_loop(0, half_rows, fill_pooled, 0)

    acc, acc2, columns = conv(x_low, w_lf, raw_low, half_rows, half_cols, column(13, two))
    halo_start(4, raw_low[0], raw_low[half_rows - 1], columns)
    act = reduce_stats(2, acc, acc2, half_rows, half_cols, column(8, two), column(10, two))
    edges = halo_finish(4, half_rows, act, False)
    fill_edges(x_mid, half_rows, half_cols, edges, 0, two)

    def fill_middle(h, c):
        put(x_mid, [h + 1], h + 1, act(raw_low[h]), edges[2], edges[3], half_cols, 0, two)
        return c
    lax.fori_loop(0, half_rows, fill_middle, 0)

    acc, acc2, columns = conv(x_mid, w_ls, raw_low, half_rows, half_cols, None)
    halo_start(5, raw_low[0], raw_low[half_rows - 1], columns)
    act_deep = reduce_stats(3, acc, acc2, half_rows, half_cols, column(9, two), column(11, two))
    deep_edges = halo_finish(5, half_rows, act_deep, True)
    fill_edges(x_join, rows, cols, deep_edges, 0, one + two)
    widen = mover(0, 0, cols, True)

    def fill_deep(h, c):
        y = jnp.dot(act_deep(raw_low[h]).astype(BF16), widen, preferred_element_type=F32)
        put(x_join, [2 * h + 1, 2 * h + 2], 2 * h + 1, y, deep_edges[2], deep_edges[3], cols, 0, one + two)
        return c
    lax.fori_loop(0, half_rows, fill_deep, 0)

    acc, acc2, columns = conv(x_join, w_df, raw_up, rows, cols, None)
    halo_start(6, raw_up[0], raw_up[rows - 1], columns)
    act_dec = reduce_stats(4, acc, acc2, rows, cols, column(2, one), column(6, one))
    dec_edges = halo_finish(6, rows, act_dec, False)
    fill_edges(x_one, rows, cols, dec_edges, 0, one)

    def fill_decoded(h, c):
        put(x_one, [h + 1], h + 1, act_dec(raw_up[h]), dec_edges[2], dec_edges[3], cols, 0, one)
        return c
    lax.fori_loop(0, rows, fill_decoded, 0)

    acc, acc2, columns = conv(x_one, w_ds, raw_up, rows, cols, None)
    act_ref = reduce_stats(5, acc, acc2, rows, cols, column(3, one), column(7, one))

    def project(h, c):
        y = jnp.concatenate([act_ref(raw_up[2 * h]), act_ref(raw_up[2 * h + 1])], axis=1).astype(BF16)
        o = jnp.dot(w_out[...], y, preferred_element_type=F32).astype(BF16)
        out[2 * h] = o[:, :LANES]
        out[2 * h + 1] = o[:, LANES:]
        return c
    lax.fori_loop(0, half_rows, project, 0)


def embedding(timestep, time_weight, bias_upper, bias_lower):
    moment = timestep[0].astype(F32)
    half_width = time_weight.shape[0] // 2
    frequencies = jnp.exp(-math.log(10000.0) * jnp.arange(half_width, dtype=F32) / half_width)
    angles = moment * frequencies
    features = jnp.concatenate([jnp.sin(angles), jnp.cos(angles)])[None, :]
    embedded = jax.nn.silu(jnp.dot(features, time_weight, precision=HIGH, preferred_element_type=F32))
    both = jnp.concatenate([bias_upper, bias_lower], axis=1)
    biases = jnp.dot(embedded, both, precision=HIGH, preferred_element_type=F32)[0]
    return biases[: bias_upper.shape[1]], biases[bias_upper.shape[1]:]


def flat(weight, channels):
    pad = channels - weight.shape[3]
    if pad:
        weight = jnp.pad(weight, ((0, 0), (0, 0), (0, 0), (0, pad)))
    return jnp.transpose(weight, (2, 0, 1, 3)).reshape(weight.shape[2], -1)


def per_device(
    noisy_image, seam_codes, timestep, time_weight, bias_upper, bias_lower,
    kernel_upper_first, kernel_upper_second, kernel_lower_first, kernel_lower_second,
    kernel_decode_first, kernel_decode_second, output_weight,
    gains_upper, shifts_upper, gains_lower, shifts_lower,
):
    tiles = lax.axis_size("tile")
    _, channels, rows, cols = noisy_image.shape
    one, two = gains_upper.shape[1], gains_lower.shape[1]
    assert lax.axis_size("split") == 2 and cols == LANES and rows * 2 == cols
    first_bias, second_bias = embedding(timestep, time_weight, bias_upper, bias_lower)
    wide = lambda v: jnp.pad(v, ((0, 0), (0, two - v.shape[1])))
    params = jnp.concatenate(
        [wide(gains_upper), wide(shifts_upper), gains_lower, shifts_lower, wide(first_bias[None]),
         second_bias[None]], axis=0).T
    image = jnp.pad(jnp.transpose(noisy_image[0], (1, 0, 2)), ((0, 0), (0, one - channels), (0, 0)))
    projection = jnp.pad(output_weight, ((0, one - channels), (0, 0)))
    widths = (one, one, one, one, two, two, one)
    depth = tiles // ROW_TILES
    plane = 2 * ROW_TILES
    vmem = pl.BlockSpec(memory_space=pltpu.VMEM)
    result = pl.pallas_call(
        functools.partial(kernel, tiles, one, two, rows, cols, channels),
        out_shape=jax.ShapeDtypeStruct((rows, one, cols), BF16),
        in_specs=[pl.BlockSpec(memory_space=pltpu.SMEM)] + [vmem] * 9,
        out_specs=vmem,
        scratch_shapes=[
            pltpu.VMEM((rows + 2, 3 * one, LANES), BF16),
            pltpu.VMEM((rows // 2 + 2, 3 * one, LANES), BF16),
            pltpu.VMEM((rows // 2 + 2, 3 * two, LANES), BF16),
            pltpu.VMEM((rows + 2, 3 * (one + two), LANES), BF16),
            pltpu.VMEM((rows, one, LANES), F32),
            pltpu.VMEM((rows // 2, two, LANES), F32),
            pltpu.VMEM((rows // 2, one, LANES), F32),
            pltpu.VMEM((6, 2 * GROUPS, LANES), F32),
            pltpu.VMEM((6, plane, 2 * GROUPS, LANES), F32),
            pltpu.VMEM((6, 2 * GROUPS, LANES), F32),
            pltpu.VMEM((6, depth, 2 * GROUPS, LANES), F32),
        ]
        + [pltpu.VMEM((3, width, LANES), BF16) for width in widths]
        + [pltpu.VMEM((6, 2, width, LANES), BF16) for width in widths]
        + [pltpu.VMEM((width, LANES), BF16) for width in widths]
        + [
            pltpu.SemaphoreType.DMA((7, 7)),
            pltpu.SemaphoreType.DMA((7, 7)),
            pltpu.SemaphoreType.DMA((6, plane + depth)),
            pltpu.SemaphoreType.DMA((6, plane + depth)),
        ],
        compiler_params=pltpu.CompilerParams(
            collective_id=0, has_side_effects=True, vmem_limit_bytes=48 * 1024 * 1024),
    )(
        seam_codes, image, params,
        flat(kernel_upper_first, one), flat(kernel_upper_second, one),
        flat(kernel_lower_first, one), flat(kernel_lower_second, two),
        flat(kernel_decode_first, one + two), flat(kernel_decode_second, one), projection,
    )
    return jnp.transpose(result[:, :channels], (1, 0, 2))[None]


def solution(mesh):
    placed = (P("tile", None, "split", None),) + (P(),) * 16
    return jax.shard_map(
        per_device, mesh=mesh, in_specs=placed, out_specs=P("tile", None, "split", None), check_vma=False,
    )
```

time: 793 us -> 153 us (0.19); the launches traced: 781 us -> 153 us
  blocking collectives: 399 us -> 0 us
  local copies, waits for them, and re-layouts: 265 us -> 8.64 us
  Pallas kernels: 0 us -> 143 us
  other arithmetic: 50.8 us -> 0.06 us
  waiting for transfers between devices: 27.1 us -> 0 us
  starting transfers between devices: 18.5 us -> 0 us
  matrix products: 15.6 us -> 0.46 us
    psum x6 -> x0, blocking collectives: 230 us -> none  [norm_act(): lax.psum((jnp.sum(grouped, axis=1), jnp.sum(jnp.square(grouped), axis=1))...]
    all_gather x24 -> x0, blocking collectives: 169 us -> none  [the longest x6 61.3 us: framed_block(): lax.all_gather(values[None, :, :, block_cols - 1], 'split', axis=0, tiled...]
    pallas_call x0 -> x1, Pallas kernels: none -> 143 us  [per_device(): pl.pallas_call(functools.partial(kernel, tiles, one, two, rows, cols, cha...]
    slice x48 -> x0, local copies, waits for them, and re-layouts: 89.7 us -> none  [the longest x15 79.6 us: apply_taps(): padded[:, row_off:row_off + height, col_off:col_off + width]]
    concatenate x7 -> x2, local copies, waits for them, and re-layouts: 61.9 us -> 0.15 us  [per_device(): jnp.concatenate([wide(gains_upper), wide(shifts_upper), gains_lower, shif...]
    unnamed x218 -> x35, local copies, waits for them, and re-layouts: 43.4 us -> 5.81 us
    concatenate x10 -> x0, other arithmetic: 30.6 us -> none  [the longest x6 19.9 us: framed_block(): jnp.concatenate([west_column[:, :, None], stacked, east_column[:, :, None...]
    ppermute x24 -> x0, waiting for transfers between devices: 27.1 us -> none  [from_behind(): return lax.ppermute(value, axis, pairs)]
  transfers between devices with their start and end apart: 24 -> 0, of which waited for: 11 -> 0; matrix products, arithmetic and copies ran while one was open for 3% -> 0% of each run, Pallas kernels for 0% -> 0%
where the time goes in v1:
time: 153 us
  Pallas kernels  143 us (93%)
  local copies, waits for them, and re-layouts  8.64 us (6%)
    pallas_call x1, Pallas kernels, per_device(): pl.pallas_call(functools.partial(kernel, tiles, one, two, rows, cols, cha...  143 us
    unnamed x35, local copies, waits for them, and re-layouts  5.81 us

profile of v1, /device:TPU:0, one launch (start us, length us, event | category | flops | bytes accessed | tf_op | source)
XLA Modules:
  0.0 152.6 jit_solution(8415663773964300968)
XLA Ops:
  0.7 0.1 copy-done
  0.8 0.2 fusion.4
  1.1 0.4 copy-done.12
  1.5 0.2 copy-done.11
  1.7 0.1 copy.59.codes
  1.8 0.1 copy.52
  2.0 0.3 fusion
  2.2 0.1 slice_bitcast_fusion.1
  2.3 0.6 copy-done.15
  2.9 0.1 copy-done.14
  3.1 0.1 copy.53
  3.2 0.1 copy.60.w_lf
  3.3 0.8 copy-done.5
  4.1 0.1 copy.54
  4.2 0.1 reshape.33.w_uf
  4.3 0.8 copy-done.6
  5.1 0.1 copy.55
  5.1 0.1 reshape.34.w_us
  5.3 0.8 copy-done.7
  6.0 0.1 copy.58
  6.1 0.1 reshape.38.w_ds
  6.2 0.7 copy-done.2
  7.0 0.2 copy.56
  7.1 0.2 copy.61.w_ls
  7.3 0.6 copy-done.3
  7.9 0.2 copy.57
  8.0 0.2 reshape.37.w_df
  8.3 0.5 copy.64
  8.8 0.1 pad.23.image
  8.9 142.6 %shard_map.163 = bf16[64,48,128]{2,1,0:T(8,128)(2,1)S(1)} custom-call(s32[16,4]{1,0:T(8,128)S(1)} %copy.59.codes, bf16[64,48,128]{2,1,0:T(8,128)(2,1)S(1)} %pad.23.image, f32[96,14]{1,0:T(8,128)S(1)} %bitcast.33, bf16[48,432]{1,0:T(8,128)(2,1)S(1)} %reshape.33.w_uf, bf16[48,432]{1,0:T(8,128)(2,1)S(1)} %reshape.34.w_us, bf16[96,432]{1,0:T(8,128)(2,1)S(1)} %copy.60.w_lf, ...), custom_call_target="tpu_custom_call" | custom-call | tf_op jit(solution)/shard_map/pallas_call | solution.py:382
  151.5 0.1 slice_bitcast_fusion
  151.5 1.1 copy.62
  (31 shorter events, 0.3 us)
Async XLA Ops:
  0.0 0.8 copy-start
  0.7 0.8 copy-start.13
  0.8 0.7 copy-start.12
  0.8 1.0 copy-start.9
  1.0 0.7 copy-start.11
  1.0 0.8 copy-start.10
  1.0 0.9 copy-start.8
  2.0 1.2 copy-start.4
  2.2 0.7 copy-start.15
  2.3 0.7 copy-start.14
  3.2 0.9 copy-start.5
  4.2 0.9 copy-start.6
  5.1 0.9 copy-start.7
  6.0 0.9 copy-start.2
  7.0 0.9 copy-start.3
  7.1 1.1 copy-start.1

commit v2 on v1

--- a/solution.py
+++ b/solution.py
@@ -26,30 +26,22 @@
     tiles, one, two, rows, cols, outputs,
     codes, image, params, w_uf, w_us, w_lf, w_ls, w_df, w_ds, w_out,
     out,
-    x_one, x_low, x_mid, x_join, raw_up, raw_low, pool_ref, stats, stats_in, stats_two, stats_two_in, *rest,
+    x_one, x_low, x_mid, x_join, raw_up, raw_low, pool_ref, stats, *rest,
 ):
     sends, recvs, inners = rest[0:7], rest[7:14], rest[14:21]
     send_sem, recv_sem, stat_send, stat_recv = rest[21:25]
     t, s = lax.axis_index("tile"), lax.axis_index("split")
-    a, b = lax.div(t, ROW_TILES), lax.rem(t, ROW_TILES)
-    depth = tiles // ROW_TILES
-    plane = 2 * ROW_TILES
+    devices = 2 * tiles
     half_rows, half_cols = rows // 2, cols // 2
 
     def across(offset):
         return lax.rem(t + offset + tiles, tiles)
 
-    def plane_peer(step):
-        place = lax.rem(b * 2 + s + step, plane)
-        return (a * ROW_TILES + lax.div(place, 2), lax.rem(place, 2))
-
-    def depth_peer(step):
-        return (lax.rem(a + step, depth) * ROW_TILES + b, s)
-
-    peers = [plane_peer(step) for step in range(1, plane)]
-    peers += [depth_peer(step) for step in range(1, depth)]
-    for offset in (ROW_TILES, -ROW_TILES, 1, -1):
-        peers += [(across(offset), 0), (across(offset), 1)]
+    def peer_at(step):
+        place = lax.rem(t * 2 + s + step, devices)
+        return (lax.div(place, 2), lax.rem(place, 2))
+
+    peers = [peer_at(step) for step in range(1, devices)]
     barrier = pltpu.get_barrier_semaphore()
     for peer in peers:
         pl.semaphore_signal(barrier, inc=1, device_id=peer, device_id_type=MESH)
@@ -58,27 +50,33 @@
     def halo_copies(e):
         send, recv, inner = sends[e], recvs[e], inners[e]
         targets = [
-            (0, (across(ROW_TILES), 0)), (0, (across(-ROW_TILES), 1)),
-            (2, (across(-1), 0)), (2, (across(-1), 1)),
-            (4, (across(1), 0)), (4, (across(1), 1)),
+            (0, 0, (across(ROW_TILES), 0)), (1, 0, (across(-ROW_TILES), 1)),
+            (2, 2, (across(-1), 0)), (2, 2, (across(-1), 1)),
+            (3, 4, (across(1), 0)), (3, 4, (across(1), 1)),
         ]
         copies = []
-        for n, (slot, peer) in enumerate(targets):
+        for n, (strip, slot, peer) in enumerate(targets):
             copies.append(pltpu.make_async_remote_copy(
-                src_ref=send.at[pl.ds(0, 2)], dst_ref=recv.at[slot + s],
+                src_ref=send.at[strip], dst_ref=recv.at[slot + s],
                 send_sem=send_sem.at[e, n], recv_sem=recv_sem.at[e, slot + s],
                 device_id=peer, device_id_type=MESH))
         copies.append(pltpu.make_async_remote_copy(
-            src_ref=send.at[2], dst_ref=inner,
+            src_ref=send.at[4], dst_ref=inner,
             send_sem=send_sem.at[e, 6], recv_sem=recv_sem.at[e, 6],
             device_id=(t, 1 - s), device_id_type=MESH))
         return copies
 
+    def facing(tile, side):
+        return lax.rem(side + 2 + codes[tile, side], 4)
+
     def halo_start(e, top, bottom, columns):
         first = jnp.full(top.shape, s, jnp.int32) == 0
-        sends[e][0] = jnp.where(first, top, bottom).astype(BF16)
-        sends[e][1] = columns.astype(BF16)
-        sends[e][2] = jnp.where(first, bottom, top).astype(BF16)
+        outer = jnp.where(first, top, bottom)
+        right = pltpu.roll(columns, 64, 1)
+        for n, (offset, side) in enumerate(((ROW_TILES, 0), (-ROW_TILES, 2), (-1, 1), (1, 3))):
+            kv = jnp.full(top.shape, facing(across(offset), side), jnp.int32)
+            sends[e][n] = jnp.where(kv == 1, right, jnp.where(kv == 3, columns, outer)).astype(BF16)
+        sends[e][4] = jnp.where(first, bottom, top).astype(BF16)
         for copy in halo_copies(e):
             copy.start()
 
@@ -86,11 +84,11 @@
         send, recv, inner = sends[e], recvs[e], inners[e]
         for n in range(6):
             pltpu.make_async_remote_copy(
-                src_ref=send.at[pl.ds(0, 2)], dst_ref=recv.at[n],
+                src_ref=send.at[0], dst_ref=recv.at[n],
                 send_sem=send_sem.at[e, n], recv_sem=recv_sem.at[e, n],
                 device_id=(t, 1 - s), device_id_type=MESH).wait()
         pltpu.make_async_remote_copy(
-            src_ref=send.at[2], dst_ref=inner,
+            src_ref=send.at[4], dst_ref=inner,
             send_sem=send_sem.at[e, 6], recv_sem=recv_sem.at[e, 6],
             device_id=(t, 1 - s), device_id_type=MESH).wait()
 
@@ -107,22 +105,17 @@
     def halo_finish(e, height, act, up):
         halo_wait(e)
         recv = recvs[e]
-        channels = recv.shape[2]
+        channels = recv.shape[1]
         lane = lanes_of(channels)
         scale = 2 if up else 1
         tall, wide = height * scale, height * 2 * scale
         strips = []
         for place, side in ((0, 2 * s), (2, 1), (4, 3)):
-            k = lax.rem(side + 2 + codes[t, side], 4)
+            k = facing(t, side)
             kv = jnp.full((channels, LANES), k, jnp.int32)
-            zero, last = recv[place, 0].astype(F32), recv[place + 1, 0].astype(F32)
-            col0, col1 = recv[place, 1].astype(F32), recv[place + 1, 1].astype(F32)
-            upper_half = lane < height
-            left = jnp.where(upper_half, col0, pltpu.roll(col1, height, 1))
-            shift = (height - 64) % LANES
-            right = jnp.where(
-                upper_half, pltpu.roll(col0, 64, 1), pltpu.roll(col1, shift, 1) if shift else col1)
-            cand = jnp.where(kv == 0, zero, jnp.where(kv == 1, right, jnp.where(kv == 2, last, left)))
+            zero, last = recv[place].astype(F32), recv[place + 1].astype(F32)
+            halves = jnp.where(lane < height, zero, pltpu.roll(last, height, 1))
+            cand = jnp.where(kv == 0, zero, jnp.where(kv == 2, last, halves))
             reverse = 1 if place == 4 else (s if place == 0 else 0)
             front = jnp.where(k < 2, 1, 0)
             flip = front + reverse - 2 * front * reverse
@@ -179,7 +172,7 @@
         zero = jnp.zeros((outs, LANES), F32)
         return lax.fori_loop(0, height // 4, body, (zero, zero, zero))
 
-    def reduce_stats(e, acc, acc2, height, wide, gain, shift):
+    def reduce_stats(e, acc, acc2, height, wide, gain, shift, meanwhile):
         channels = acc.shape[0]
         size = channels // GROUPS
         g = lax.broadcasted_iota(jnp.int32, (GROUPS, channels), 0)
@@ -188,32 +181,19 @@
         gt = lax.broadcasted_iota(jnp.int32, (channels, GROUPS), 1)
         ct = lax.broadcasted_iota(jnp.int32, (channels, GROUPS), 0)
         spread_out = jnp.where((ct >= gt * size) & (ct < gt * size + size), 1.0, 0.0).astype(F32)
-        stats[e, pl.ds(0, GROUPS)] = jnp.dot(member, acc, precision=HIGH, preferred_element_type=F32)
-        stats[e, pl.ds(GROUPS, GROUPS)] = jnp.dot(member, acc2, precision=HIGH, preferred_element_type=F32)
-        copies = []
-        for step in range(1, plane):
-            copies.append(pltpu.make_async_remote_copy(
-                src_ref=stats.at[e], dst_ref=stats_in.at[e, step],
-                send_sem=stat_send.at[e, step], recv_sem=stat_recv.at[e, step],
-                device_id=plane_peer(step), device_id_type=MESH))
-        for copy in copies:
-            copy.start()
-        total = stats[e]
-        for step, copy in enumerate(copies):
-            copy.wait()
-            total = total + stats_in[e, step + 1]
-        stats_two[e] = total
-        copies = []
-        for step in range(1, depth):
-            copies.append(pltpu.make_async_remote_copy(
-                src_ref=stats_two.at[e], dst_ref=stats_two_in.at[e, step],
-                send_sem=stat_send.at[e, plane + step], recv_sem=stat_recv.at[e, plane + step],
-                device_id=depth_peer(step), device_id_type=MESH))
-        for copy in copies:
-            copy.start()
-        for step, copy in enumerate(copies):
-            copy.wait()
-            total = total + stats_two_in[e, step + 1]
+        stats[e, 0, pl.ds(0, GROUPS)] = jnp.dot(member, acc, precision=HIGH, preferred_element_type=F32)
+        stats[e, 0, pl.ds(GROUPS, GROUPS)] = jnp.dot(member, acc2, precision=HIGH, preferred_element_type=F32)
+        for step in range(1, devices):
+            pltpu.make_async_remote_copy(
+                src_ref=stats.at[e, 0], dst_ref=stats.at[e, step],
+                send_sem=stat_send.at[e], recv_sem=stat_recv.at[e],
+                device_id=peer_at(step), device_id_type=MESH).start()
+        meanwhile()
+        arrived = stats.at[e, pl.ds(1, devices - 1)]
+        pltpu.make_async_remote_copy(
+            src_ref=arrived, dst_ref=arrived, send_sem=stat_send.at[e], recv_sem=stat_recv.at[e],
+            device_id=peer_at(1), device_id_type=MESH).wait()
+        total = jnp.sum(stats[e], axis=0)
         total = jnp.where(lanes_of(2 * GROUPS) < wide, total, 0.0)
         means = jnp.sum(total, axis=1, keepdims=True) * (1.0 / (height * wide * size * 2 * tiles))
         mean = means[:GROUPS]
@@ -244,7 +224,7 @@
     def image_columns(h, columns):
         return columns_with(columns, image[h].astype(F32), h, cols)
 
-    columns = lax.fori_loop(0, rows, image_columns, jnp.zeros((one, LANES), F32))
+    columns = lax.fori_loop(0, rows, image_columns, jnp.zeros((one, LANES), F32), unroll=8)
     halo_start(0, image[0].astype(F32), image[rows - 1].astype(F32), columns)
     edges = halo_finish(0, rows, same, False)
     fill_edges(x_one, rows, cols, edges, 0, one)
@@ -252,22 +232,22 @@
     def fill_image(h, c):
         put(x_one, [h + 1], h + 1, image[h].astype(F32), edges[2], edges[3], cols, 0, one)
         return c
-    lax.fori_loop(0, rows, fill_image, 0)
+    lax.fori_loop(0, rows, fill_image, 0, unroll=8)
 
     acc, acc2, columns = conv(x_one, w_uf, raw_up, rows, cols, column(12, one))
-    halo_start(1, raw_up[0], raw_up[rows - 1], columns)
-    act = reduce_stats(0, acc, acc2, rows, cols, column(0, one), column(4, one))
+    act = reduce_stats(0, acc, acc2, rows, cols, column(0, one), column(4, one),
+        lambda: halo_start(1, raw_up[0], raw_up[rows - 1], columns))
     edges = halo_finish(1, rows, act, False)
     fill_edges(x_one, rows, cols, edges, 0, one)
 
     def fill_first(h, c):
         put(x_one, [h + 1], h + 1, act(raw_up[h]), edges[2], edges[3], cols, 0, one)
         return c
-    lax.fori_loop(0, rows, fill_first, 0)
+    lax.fori_loop(0, rows, fill_first, 0, unroll=8)
 
     acc, acc2, columns = conv(x_one, w_us, raw_up, rows, cols, None)
-    halo_start(2, raw_up[0], raw_up[rows - 1], columns)
-    act_skip = reduce_stats(1, acc, acc2, rows, cols, column(1, one), column(5, one))
+    act_skip = reduce_stats(1, acc, acc2, rows, cols, column(1, one), column(5, one),
+        lambda: halo_start(2, raw_up[0], raw_up[rows - 1], columns))
     skip_edges = halo_finish(2, rows, act_skip, False)
     fill_edges(x_join, rows, cols, skip_edges, two, one + two)
     i = lax.broadcasted_iota(jnp.int32, (LANES, LANES), 0)
@@ -282,7 +262,7 @@
             pooled = pooled + jnp.dot(y.astype(BF16), pooling, preferred_element_type=F32)
         pool_ref[h] = pooled
         return columns_with(columns, pooled, h, half_cols)
-    columns = lax.fori_loop(0, half_rows, fill_skip, jnp.zeros((one, LANES), F32))
+    columns = lax.fori_loop(0, half_rows, fill_skip, jnp.zeros((one, LANES), F32), unroll=8)
     halo_start(3, pool_ref[0], pool_ref[half_rows - 1], columns)
     edges = halo_finish(3, half_rows, same, False)
     fill_edges(x_low, half_rows, half_cols, edges, 0, one)
@@ -290,22 +270,22 @@
     def fill_pooled(h, c):
         put(x_low, [h + 1], h + 1, pool_ref[h], edges[2], edges[3], half_cols, 0, one)
         return c
-    lax.fori_loop(0, half_rows, fill_pooled, 0)
+    lax.fori_loop(0, half_rows, fill_pooled, 0, unroll=8)
 
     acc, acc2, columns = conv(x_low, w_lf, raw_low, half_rows, half_cols, column(13, two))
-    halo_start(4, raw_low[0], raw_low[half_rows - 1], columns)
-    act = reduce_stats(2, acc, acc2, half_rows, half_cols, column(8, two), column(10, two))
+    act = reduce_stats(2, acc, acc2, half_rows, half_cols, column(8, two), column(10, two),
+        lambda: halo_start(4, raw_low[0], raw_low[half_rows - 1], columns))
     edges = halo_finish(4, half_rows, act, False)
     fill_edges(x_mid, half_rows, half_cols, edges, 0, two)
 
     def fill_middle(h, c):
         put(x_mid, [h + 1], h + 1, act(raw_low[h]), edges[2], edges[3], half_cols, 0, two)
         return c
-    lax.fori_loop(0, half_rows, fill_middle, 0)
+    lax.fori_loop(0, half_rows, fill_middle, 0, unroll=8)
 
     acc, acc2, columns = conv(x_mid, w_ls, raw_low, half_rows, half_cols, None)
-    halo_start(5, raw_low[0], raw_low[half_rows - 1], columns)
-    act_deep = reduce_stats(3, acc, acc2, half_rows, half_cols, column(9, two), column(11, two))
+    act_deep = reduce_stats(3, acc, acc2, half_rows, half_cols, column(9, two), column(11, two),
+        lambda: halo_start(5, raw_low[0], raw_low[half_rows - 1], columns))
     deep_edges = halo_finish(5, half_rows, act_deep, True)
     fill_edges(x_join, rows, cols, deep_edges, 0, one + two)
     widen = mover(0, 0, cols, True)
@@ -314,21 +294,21 @@
         y = jnp.dot(act_deep(raw_low[h]).astype(BF16), widen, preferred_element_type=F32)
         put(x_join, [2 * h + 1, 2 * h + 2], 2 * h + 1, y, deep_edges[2], deep_edges[3], cols, 0, one + two)
         return c
-    lax.fori_loop(0, half_rows, fill_deep, 0)
+    lax.fori_loop(0, half_rows, fill_deep, 0, unroll=8)
 
     acc, acc2, columns = conv(x_join, w_df, raw_up, rows, cols, None)
-    halo_start(6, raw_up[0], raw_up[rows - 1], columns)
-    act_dec = reduce_stats(4, acc, acc2, rows, cols, column(2, one), column(6, one))
+    act_dec = reduce_stats(4, acc, acc2, rows, cols, column(2, one), column(6, one),
+        lambda: halo_start(6, raw_up[0], raw_up[rows - 1], columns))
     dec_edges = halo_finish(6, rows, act_dec, False)
     fill_edges(x_one, rows, cols, dec_edges, 0, one)
 
     def fill_decoded(h, c):
         put(x_one, [h + 1], h + 1, act_dec(raw_up[h]), dec_edges[2], dec_edges[3], cols, 0, one)
         return c
-    lax.fori_loop(0, rows, fill_decoded, 0)
+    lax.fori_loop(0, rows, fill_decoded, 0, unroll=8)
 
     acc, acc2, columns = conv(x_one, w_ds, raw_up, rows, cols, None)
-    act_ref = reduce_stats(5, acc, acc2, rows, cols, column(3, one), column(7, one))
+    act_ref = reduce_stats(5, acc, acc2, rows, cols, column(3, one), column(7, one), lambda: None)
 
     def project(h, c):
         y = jnp.concatenate([act_ref(raw_up[2 * h]), act_ref(raw_up[2 * h + 1])], axis=1).astype(BF16)
@@ -336,7 +316,7 @@
         out[2 * h] = o[:, :LANES]
         out[2 * h + 1] = o[:, LANES:]
         return c
-    lax.fori_loop(0, half_rows, project, 0)
+    lax.fori_loop(0, half_rows, project, 0, unroll=8)
 
 
 def embedding(timestep, time_weight, bias_upper, bias_lower):
@@ -376,8 +356,6 @@
     image = jnp.pad(jnp.transpose(noisy_image[0], (1, 0, 2)), ((0, 0), (0, one - channels), (0, 0)))
     projection = jnp.pad(output_weight, ((0, one - channels), (0, 0)))
     widths = (one, one, one, one, two, two, one)
-    depth = tiles // ROW_TILES
-    plane = 2 * ROW_TILES
     vmem = pl.BlockSpec(memory_space=pltpu.VMEM)
     result = pl.pallas_call(
         functools.partial(kernel, tiles, one, two, rows, cols, channels),
@@ -392,19 +370,16 @@
             pltpu.VMEM((rows, one, LANES), F32),
             pltpu.VMEM((rows // 2, two, LANES), F32),
             pltpu.VMEM((rows // 2, one, LANES), F32),
-            pltpu.VMEM((6, 2 * GROUPS, LANES), F32),
-            pltpu.VMEM((6, plane, 2 * GROUPS, LANES), F32),
-            pltpu.VMEM((6, 2 * GROUPS, LANES), F32),
-            pltpu.VMEM((6, depth, 2 * GROUPS, LANES), F32),
+            pltpu.VMEM((6, 2 * tiles, 2 * GROUPS, LANES), F32),
         ]
-        + [pltpu.VMEM((3, width, LANES), BF16) for width in widths]
-        + [pltpu.VMEM((6, 2, width, LANES), BF16) for width in widths]
+        + [pltpu.VMEM((5, width, LANES), BF16) for width in widths]
+        + [pltpu.VMEM((6, width, LANES), BF16) for width in widths]
         + [pltpu.VMEM((width, LANES), BF16) for width in widths]
         + [
             pltpu.SemaphoreType.DMA((7, 7)),
             pltpu.SemaphoreType.DMA((7, 7)),
-            pltpu.SemaphoreType.DMA((6, plane + depth)),
-            pltpu.SemaphoreType.DMA((6, plane + depth)),
+            pltpu.SemaphoreType.DMA((6,)),
+            pltpu.SemaphoreType.DMA((6,)),
         ],
         compiler_params=pltpu.CompilerParams(
             collective_id=0, has_side_effects=True, vmem_limit_bytes=48 * 1024 * 1024),

time: 153 us -> 117 us (0.76)
  Pallas kernels: 143 us -> 106 us
    pallas_call x1, Pallas kernels: 143 us -> 106 us  [per_device(): pl.pallas_call(functools.partial(kernel, tiles, one, two, rows, cols, cha...]
where the time goes in v2:
time: 117 us; the launch traced here: 116 us
  Pallas kernels  106 us (91%)
  local copies, waits for them, and re-layouts  8.64 us (7%)
    pallas_call x1, Pallas kernels, per_device(): pl.pallas_call(functools.partial(kernel, tiles, one, two, rows, cols, cha...  106 us
    unnamed x35, local copies, waits for them, and re-layouts  5.81 us

profile of v2, /device:TPU:0, one launch (start us, length us, event | category | flops | bytes accessed | tf_op | source)
XLA Modules:
  0.0 116.3 jit_solution(5790289622530077575)
XLA Ops:
  0.7 0.1 copy-done
  0.8 0.2 fusion.4
  1.1 0.4 copy-done.12
  1.5 0.2 copy-done.11
  1.7 0.1 copy.59.codes
  1.8 0.1 copy.52
  2.0 0.3 fusion
  2.2 0.1 slice_bitcast_fusion.1
  2.3 0.6 copy-done.15
  2.9 0.1 copy-done.14
  3.1 0.1 copy.53
  3.2 0.1 copy.60.w_lf
  3.3 0.8 copy-done.5
  4.1 0.1 copy.54
  4.2 0.1 reshape.33.w_uf
  4.3 0.8 copy-done.6
  5.1 0.1 copy.55
  5.1 0.1 reshape.34.w_us
  5.3 0.8 copy-done.7
  6.0 0.1 copy.58
  6.1 0.1 reshape.38.w_ds
  6.2 0.7 copy-done.2
  7.0 0.2 copy.56
  7.1 0.2 copy.61.w_ls
  7.3 0.6 copy-done.3
  7.9 0.2 copy.57
  8.0 0.2 reshape.37.w_df
  8.3 0.5 copy.64
  8.8 0.1 pad.23.image
  8.9 106.4 %shard_map.163 = bf16[64,48,128]{2,1,0:T(8,128)(2,1)S(1)} custom-call(s32[16,4]{1,0:T(8,128)S(1)} %copy.59.codes, bf16[64,48,128]{2,1,0:T(8,128)(2,1)S(1)} %pad.23.image, f32[96,14]{1,0:T(8,128)S(1)} %bitcast.33, bf16[48,432]{1,0:T(8,128)(2,1)S(1)} %reshape.33.w_uf, bf16[48,432]{1,0:T(8,128)(2,1)S(1)} %reshape.34.w_us, bf16[96,432]{1,0:T(8,128)(2,1)S(1)} %copy.60.w_lf, ...), custom_call_target="tpu_custom_call" | custom-call | tf_op jit(solution)/shard_map/pallas_call | solution.py:360
  115.2 0.1 slice_bitcast_fusion
  115.3 1.1 copy.62
  (31 shorter events, 0.3 us)
Async XLA Ops:
  0.0 0.8 copy-start
  0.7 0.8 copy-start.13
  0.8 0.7 copy-start.12
  0.8 1.0 copy-start.9
  1.0 0.7 copy-start.11
  1.0 0.8 copy-start.10
  1.0 0.9 copy-start.8
  2.0 1.2 %copy-start.4 = (bf16[3,3,96,48]{2,3,1,0:T(8,128)(2,1)S(1)}, bf16[3,3,96,48]{2,3,1,0:T(8,128)(2,1)}, u32[]{:S(2)}) copy-start(bf16[3,3,96,48]{2,3,1,0:T(8,128)(2,1)} %param.25) | copy-start | bytes 248836
  2.2 0.7 copy-start.15
  2.3 0.7 copy-start.14
  3.2 0.9 copy-start.5
  4.2 0.9 copy-start.6
  5.1 0.9 copy-start.7
  6.0 0.9 copy-start.2
  7.0 0.9 copy-start.3
  7.1 1.1 copy-start.1
